TPU v7x, 768 devices: a whole 4x8x12 slice. The times are simulated.
768 devices in a mesh: row: 24 (over z_lo, y), col: 32 (over x, z_hi, core).
Axes of the slice: x: 4, y: 8, z: 12 (z_hi: 4, z_lo: 3; z = z_hi * 3 + z_lo), core: 2. Of those that a mesh axis runs over, the one named last changes fastest.
Arguments:
- amplitudes: bfloat16 [768, 49152], P('row', 'col'), may hold values from -6 to 6
- amp_tiles: int32 [12, 768], P(None, 'col'), may hold values from 0 to 1, as said below
- integrals: bfloat16 [30720, 49152], P('row', 'col'), may hold values from -0.0390625 to 0.0390625
- int_tiles: int32 [480, 768], P('row', 'col'), may hold values from 0 to 1, as said below
- prior: float32 [768, 30720], P('col', 'row'), may hold values from -6 to 6
Outputs:
- ladder: float32 [768, 30720], P('col', 'row')
Inputs may be any that keep to these rules, and one draw needn't show every extreme that they name: `amp_tiles`: each entry flags one tile as nonzero (1) or zero (0). `int_tiles`: each entry flags one tile as nonzero (1) or zero (0); some rows of tiles are zero throughout.
All inputs are finite; a program needn't handle non-finite values.
Results may differ from a plain program's by a relative error of at most 0.0003.
Values may be sent and summed in bfloat16 or wider, within the bound.
No kernel may reach another device: no remote copies, remote signals or barrier semaphores. Data moves between devices by JAX's collectives and lax.ppermute only.
A program may use at most 64 MiB of HBM per device.

v0:
```python
import jax
import jax.numpy as jnp
from jax import lax
from jax.sharding import PartitionSpec as P


def mask_tiles(values, row_mask):
    row_total = values.shape[0]
    tile_count = row_mask.shape[1]
    shaped = values.reshape(row_total, tile_count, values.shape[1] // tile_count)
    return (shaped * row_mask[:, :, None].astype(values.dtype)).reshape(values.shape)


def contract(amp_rows, v_slab):
    return lax.dot_general(
        amp_rows, v_slab, (((1,), (1,)), ((), ())), preferred_element_type=jnp.float32
    )


def on_device(amplitudes, amp_tiles, integrals, int_tiles, prior):
    local_rows = amplitudes.shape[0]
    tile_size = amplitudes.shape[1] // amp_tiles.shape[1]
    expanded = jnp.repeat(amp_tiles, tile_size, axis=0)
    row_start = lax.axis_index("row") * local_rows
    row_mask = lax.dynamic_slice_in_dim(expanded, row_start, local_rows, 0)
    masked_amps = mask_tiles(amplitudes, row_mask)
    ab_tiles = int_tiles.shape[0]
    cd_tiles = int_tiles.shape[1]
    v_slab = (
        integrals.reshape(ab_tiles, tile_size, cd_tiles, tile_size)
        * int_tiles[:, None, :, None].astype(jnp.bfloat16)
    ).reshape(integrals.shape)
    partial_sums = contract(lax.all_gather(masked_amps, "row", axis=0, tiled=True), v_slab)
    summed = lax.psum_scatter(partial_sums, "col", scatter_dimension=0, tiled=True)
    return prior + summed


def solution(mesh):
    in_specs = (P("row", "col"), P(None, "col"), P("row", "col"), P("row", "col"), P("col", "row"))
    out_specs = P("col", "row")
    return jax.shard_map(
        on_device, mesh=mesh, in_specs=in_specs, out_specs=out_specs, check_vma=False
    )
```

profile of v0, /device:TPU:1, one launch (start us, length us, event | category | flops | bytes accessed | tf_op | source)
XLA Modules:
  0.0 284.6 jit_solution(3172683770216395749)
XLA Ops:
  6.5 0.0 all-gather.2.cloned.1.call-start
  6.5 0.7 broadcast_in_dim.2
  7.3 0.2 mul.26
  7.5 0.2 mul.27
  7.6 1.6 mul.28
  9.2 0.0 all-gather.2.cloned.1.call-update
  9.2 0.0 reduce-scatter.2.cloned.1.call-start
  9.3 0.7 convert_element_type.9
  10.0 4.1 %mul.29 = bf16[20,64,24,64]{3,2,1,0:T(8,128)(2,1)} broadcast(bf16[20,24]{1,0:T(8,128)(2,1)S(1)} %convert_element_type.9), dimensions={0,2} | broadcast | bytes 3933120 | tf_op jit(solution)/shard_map/mul | solution.py:30
  14.1 11.1 %mul.30 = bf16[1280,1536]{1,0:T(8,128)(2,1)} reshape(bf16[20,64,24,64]{3,2,1,0:T(8,128)(2,1)} %mul.29) | data formatting | bytes 7864320 | tf_op jit(solution)/shard_map/mul | solution.py:30
  25.2 93.4 %all-gather.2.cloned.1.call-done = bf16[768,1536]{1,0:T(8,128)(2,1)} async-done(((bf16[32,1536]{1,0:T(8,128)(2,1)}), bf16[768,1536]{1,0:T(8,128)(2,1)}) %all-gather.2.cloned.1.call-update) | async-done | bytes 2359312 | tf_op jit(solution)/shard_map/all_gather | solution.py:33
  118.7 9.1 %fusion = f32[768,1280]{1,0:T(8,128)} fusion(bf16[768,1536]{1,0:T(8,128)(2,1)} %all-gather.2.cloned.1.call-done, bf16[1280,1536]{1,0:T(8,128)(2,1)} %param.7, bf16[1280,1536]{1,0:T(8,128)(2,1)} %mul.30), kind=kOutput, calls=%fused_computation | convolution fusion | flops 3021864960 | bytes 14155776 | tf_op jit(solution)/shard_map/dot_general | solution.py:15
  127.8 0.0 copy-start
  127.8 0.0 reduce-scatter.2.cloned.1.call-update
  127.8 148.4 %reduce-scatter.2.cloned.1.call-done = f32[24,1280]{1,0:T(8,128)} async-done(((f32[768,1280]{1,0:T(8,128)}), f32[24,1280]{1,0:T(8,128)}) %reduce-scatter.2.cloned.1.call-update) | async-done | bytes 122896 | tf_op jit(solution)/shard_map/reduce_scatter | solution.py:34
  276.2 0.0 copy-done
  276.2 1.6 add.9
  (1 shorter events, 0.0 us)
Async XLA Ops:
  6.5 112.1 %all-gather.2.cloned.1.call-start = ((), (), s32[]{:S(2)}) async-start(), calls=%async_computation.1 | async-start | bytes 2457600 | tf_op jit(solution)/shard_map/all_gather | solution.py:33
  9.2 266.9 %reduce-scatter.2.cloned.1.call-start = ((), (), s32[]{:S(2)}) async-start(), calls=%async_computation.2 | async-start | bytes 4055040 | tf_op jit(solution)/shard_map/reduce_scatter | solution.py:34
  127.8 148.4 %copy-start = (f32[24,1280]{1,0:T(8,128)S(1)}, f32[24,1280]{1,0:T(8,128)}, u32[]{:S(2)}) copy-start(f32[24,1280]{1,0:T(8,128)} %param.9) | copy-start | bytes 368644
Sparse Core Ops, SparseCore 0:
  9.7 108.8 all-gather.1
  127.9 148.2 reduce-scatter.1
where the time goes:
time: 285 us
  waiting for transfers between devices  242 us (85%)
  local copies, waits for them, and re-layouts  16.3 us (6%)
  between operations  13.4 us (5%)
  matrix products  9.09 us (3%)
  other arithmetic  3.85 us (1%)
    reduce_scatter x1, waiting for transfers between devices, on_device(): lax.psum_scatter(partial_sums, 'col', scatter_dimension=0, tiled=True)  148 us
    all_gather x1, waiting for transfers between devices, on_device(): lax.all_gather(masked_amps, 'row', axis=0, tiled=True)  93.4 us
    mul x2, local copies, waits for them, and re-layouts, on_device(): integrals.reshape(ab_tiles, tile_size, cd_tiles, tile_size)  15.3 us
    dot_general x1, matrix products, contract(): lax.dot_general(amp_rows, v_slab, (((1,), (1,)), ((), ())), preferred_ele...  9.09 us
  transfers between devices with their start and end apart: 2, of which 2 were waited for; matrix products, arithmetic and copies ran while one was open for 6% of the time, Pallas kernels for 0%

commit v1 on v0

v1 whole, which is shorter than its diff:
```python
import jax
import jax.numpy as jnp
from jax import lax
from jax.experimental import pallas as pl
from jax.experimental.pallas import tpu as pltpu
from jax.sharding import Mesh, PartitionSpec as P

AXES = ("zlo", "y", "x", "zhi", "core")
SIZES = (3, 8, 4, 4, 2)
ROW = ("zlo", "y")
COL = ("x", "zhi", "core")
TILE = 64
BLOCK = 256

AMP_SCALE = 2.0**13
X_SCALE = 2.0**6
Z_SCALE = 2.0**4


def product_kernel(amps_ref, tiles_ref, ints_ref, out_ref, mask_ref):
    @pl.when(pl.program_id(0) == 0)
    def _():
        count, width = tiles_ref.shape[1], ints_ref.shape[1]
        tile_of = lax.shift_right_logical(
            lax.broadcasted_iota(jnp.int32, (count, width), 1), TILE.bit_length() - 1
        )
        spread = (tile_of == lax.broadcasted_iota(jnp.int32, (count, width), 0)).astype(jnp.bfloat16)
        mask_ref[...] = jnp.dot(
            tiles_ref[...].astype(jnp.bfloat16), spread, preferred_element_type=jnp.float32
        )

    first = pl.program_id(0) * (BLOCK // TILE)
    parts = []
    for k in range(BLOCK // TILE):
        row = mask_ref[pl.ds(first + k, 1), :].astype(jnp.bfloat16)
        parts.append(ints_ref[k * TILE : (k + 1) * TILE, :] * row)
    masked = jnp.concatenate(parts, axis=0)
    out_ref[...] = lax.dot_general(
        amps_ref[...], masked, (((1,), (1,)), ((), ())), preferred_element_type=jnp.float32
    )


def product(amps, int_tiles, integrals):
    rows, depth = amps.shape
    ab = integrals.shape[0]
    return pl.pallas_call(
        product_kernel,
        grid=(ab // BLOCK,),
        in_specs=[
            pl.BlockSpec((rows, depth), lambda b: (0, 0)),
            pl.BlockSpec(int_tiles.shape, lambda b: (0, 0)),
            pl.BlockSpec((BLOCK, depth), lambda b: (b, 0)),
        ],
        out_specs=pl.BlockSpec((rows, BLOCK), lambda b: (0, b)),
        out_shape=jax.ShapeDtypeStruct((rows, ab), jnp.float32),
        scratch_shapes=[pltpu.VMEM((int_tiles.shape[0], depth), jnp.float32)],
        compiler_params=pltpu.CompilerParams(vmem_limit_bytes=40 * 2**20),
        cost_estimate=pl.CostEstimate(
            flops=2 * rows * ab * depth, bytes_accessed=2 * (rows + ab) * depth + 4 * rows * ab, transcendentals=0
        ),
    )(amps, int_tiles, integrals)


def on_device(amplitudes, amp_tiles, integrals, int_tiles, prior):
    f16, f32 = jnp.float16, jnp.float32
    local_rows, depth = amplitudes.shape
    ab = integrals.shape[0]
    own_rows = prior.shape[0]
    core, x, zhi = lax.axis_index("core"), lax.axis_index("x"), lax.axis_index("zhi")
    row = lax.axis_index(ROW)
    n_x, n_zhi, n_core = lax.axis_size("x"), lax.axis_size("zhi"), lax.axis_size("core")

    flags = lax.dynamic_slice_in_dim(amp_tiles, row * local_rows // TILE, 1, 0)
    mask = jnp.repeat(flags.astype(f32) * AMP_SCALE, TILE, axis=1)
    sent = (amplitudes.astype(f32) * mask).astype(f16)
    near = lax.all_gather(sent, "zlo", axis=0, tiled=False)
    amps = lax.all_gather(near, "y", axis=1, tiled=False)
    amps = amps.astype(jnp.bfloat16).reshape(n_x, n_zhi, n_core, own_rows, depth)
    amps = amps.transpose(2, 0, 1, 3, 4).reshape(n_core, n_x * n_zhi * own_rows, depth)

    other = product(lax.dynamic_index_in_dim(amps, 1 - core, 0, False), int_tiles, integrals)
    crossing = lax.ppermute(other, "core", [(0, 1), (1, 0)])
    mine = product(lax.dynamic_index_in_dim(amps, core, 0, False), int_tiles, integrals)
    total = ((mine + crossing) * (X_SCALE / AMP_SCALE)).reshape(n_x, n_zhi * own_rows, ab)

    got = lax.all_to_all(total.astype(f16), "x", 0, 0, tiled=True)
    total = got.astype(f32).sum(0) * (Z_SCALE / X_SCALE)
    total = total.reshape(n_zhi, own_rows, ab)
    got = lax.all_to_all(total.astype(f16), "zhi", 0, 0, tiled=True)
    return prior + got.astype(f32).sum(0) * (1 / Z_SCALE)


def solution(mesh):
    parts = Mesh(mesh.devices.reshape(SIZES), AXES)
    in_specs = (P(ROW, COL), P(None, COL), P(ROW, COL), P(ROW, COL), P(COL, ROW))
    return jax.shard_map(
        on_device, mesh=parts, in_specs=in_specs, out_specs=P(COL, ROW), check_vma=False
    )
```

time: 285 us -> 106 us (0.37)
  waiting for transfers between devices: 242 us -> 0.7 us
  blocking collectives: 0 us -> 79 us
  local copies, waits for them, and re-layouts: 16.3 us -> 2.45 us
  between operations: 13.4 us -> 0.1 us
  starting transfers between devices: 0.04 us -> 12.7 us
  matrix products: 9.09 us -> 0 us
  Pallas kernels: 0 us -> 5.71 us
    reduce_scatter x1 -> x0, waiting for transfers between devices: 148 us -> none  [on_device(): lax.psum_scatter(partial_sums, 'col', scatter_dimension=0, tiled=True)]
    all_gather x1 -> x0, waiting for transfers between devices: 93.4 us -> none  [on_device(): lax.all_gather(masked_amps, 'row', axis=0, tiled=True)]
    all_to_all x0 -> x2, blocking collectives: none -> 40.7 us  [the longest x1 24.5 us: on_device(): got = lax.all_to_all(total.astype(f16), 'zhi', 0, 0, tiled=True)]
    all_gather x0 -> x2, blocking collectives: none -> 38.3 us  [the longest x1 27.5 us: on_device(): amps = lax.all_gather(near, 'y', axis=1, tiled=False)]
    mul x4 -> x0, local copies, waits for them, and re-layouts: 15.6 us -> none  [the longest x2 15.3 us: on_device(): integrals.reshape(ab_tiles, tile_size, cd_tiles, tile_size)]
    ppermute x0 -> x1, starting transfers between devices: none -> 12.7 us  [on_device(): crossing = lax.ppermute(other, 'core', [(0, 1), (1, 0)])]
    dot_general x1 -> x0, matrix products: 9.09 us -> none  [contract(): lax.dot_general(amp_rows, v_slab, (((1,), (1,)), ((), ())), preferred_ele...]
    pallas_call x0 -> x2, Pallas kernels: none -> 5.71 us  [product(): pl.pallas_call(product_kernel, grid=(ab // BLOCK,), in_specs=[pl.BlockSpe...]
  transfers between devices with their start and end apart: 2 -> 1, of which waited for: 2 -> 1; matrix products, arithmetic and copies ran while one was open for 6% -> 0% of each run, Pallas kernels for 0% -> 3%
where the time goes in v1:
time: 106 us; the launch traced here: 104 us
  blocking collectives  79 us (75%)
  starting transfers between devices  12.7 us (12%)
  Pallas kernels  5.71 us (5%)
  other arithmetic  3.14 us (3%)
  local copies, waits for them, and re-layouts  2.45 us (2%)
    all_gather x1, blocking collectives, on_device(): amps = lax.all_gather(near, 'y', axis=1, tiled=False)  27.5 us
    all_to_all x1, blocking collectives, on_device(): got = lax.all_to_all(total.astype(f16), 'zhi', 0, 0, tiled=True)  24.5 us
    all_to_all x1, blocking collectives, on_device(): got = lax.all_to_all(total.astype(f16), 'x', 0, 0, tiled=True)  16.3 us
    ppermute x1, starting transfers between devices, on_device(): crossing = lax.ppermute(other, 'core', [(0, 1), (1, 0)])  12.7 us
    all_gather x1, blocking collectives, on_device(): near = lax.all_gather(sent, 'zlo', axis=0, tiled=False)  10.8 us
    pallas_call x2, Pallas kernels, product(): pl.pallas_call(product_kernel, grid=(ab // BLOCK,), in_specs=[pl.BlockSpe...  5.71 us
  transfers between devices with their start and end apart: 1, of which 1 were waited for; matrix products, arithmetic and copies ran while one was open for 0% of the time, Pallas kernels for 3%

profile of v1, /device:TPU:1, one launch (start us, length us, event | category | flops | bytes accessed | tf_op | source)
XLA Modules:
  0.0 103.8 jit_solution(11449208537594050962)
XLA Ops:
  0.0 0.7 fusion.2
  0.7 0.1 broadcast_in_dim.5
  0.8 0.1 broadcast_in_dim.6
  0.8 0.9 multiply_convert_fusion.2
  1.8 10.8 %all-gather = f16[96,1536]{1,0:T(8,128)(2,1)S(1)} all-gather(f16[32,1536]{1,0:T(8,128)(2,1)S(1)} %multiply_convert_fusion.2), channel_id=2, replica_groups=mesh['zlo'=3,'y'=8,'x'=4,'zhi'=4,'core'=2] {'zlo'}, dimensions={0}, use_global_device_ids=true | all-gather | bytes 393216 | tf_op jit(solution)/shard_map/all_gather | solution.py:76
  12.6 27.5 %all-gather.3 = f16[3,256,1536]{2,1,0:T(8,128)(2,1)S(1)} all-gather(f16[3,32,1536]{2,1,0:T(8,128)(2,1)S(1)} %bitcast.16), channel_id=3, replica_groups=mesh['zlo'=3,'y'=8,'x'=4,'zhi'=4,'core'=2] {'y'}, dimensions={1}, use_global_device_ids=true | all-gather | bytes 2654208 | tf_op jit(solution)/shard_map/all_gather | solution.py:77
  40.0 0.4 convert_element_type.40
  40.4 0.2 copy.7
  40.7 0.0 copy-start
  40.7 0.0 copy-start.1
  40.7 0.2 dynamic-slice_bitcast_fusion
  40.8 1.9 %copy-done = bf16[1280,1536]{1,0:T(8,128)(2,1)S(1)} copy-done((bf16[1280,1536]{1,0:T(8,128)(2,1)S(1)}, bf16[1280,1536]{1,0:T(8,128)(2,1)}, u32[]{:S(2)}) %copy-start) | copy-done | bytes 3932184
  42.8 0.0 copy-done.1
  42.8 2.8 %shard_map.56 = f32[384,1280]{1,0:T(8,128)S(1)} custom-call(bf16[384,1536]{1,0:T(8,128)(2,1)S(1)} %get-tuple-element.5.amps_ref, s32[20,24]{1,0:T(8,128)S(1)} %copy-done.1, bf16[1280,1536]{1,0:T(8,128)(2,1)S(1)} %copy-done), custom_call_target="tpu_custom_call" | custom-call | flops 1509949440 | bytes 7077888 | tf_op jit(solution)/shard_map/pallas_call | solution.py:46
  45.6 12.7 %collective-permute-start = (f32[384,1280]{1,0:T(8,128)S(1)}, f32[384,1280]{1,0:T(8,128)S(1)}, u32[]{:S(2)}, u32[]{:S(2)}) collective-permute-start(f32[384,1280]{1,0:T(8,128)S(1)} %shard_map.56), channel_id=1, source_target_pairs={{0,1},{1,0},{2,3},{3,2},{4,5},{5,4},{6,7},{7,6},{8,9},{9,8},{10,11... | collective-permute-start | bytes 5898248 | tf_op jit(solution)/shard_map/ppermute | solution.py:82
  58.3 2.9 %shard_map.55 = f32[384,1280]{1,0:T(8,128)S(1)} custom-call(bf16[384,1536]{1,0:T(8,128)(2,1)S(1)} %get-tuple-element.6.amps_ref, s32[20,24]{1,0:T(8,128)S(1)} %copy-done.1, bf16[1280,1536]{1,0:T(8,128)(2,1)S(1)} %copy-done), custom_call_target="tpu_custom_call" | custom-call | flops 1509949440 | bytes 7077888 | tf_op jit(solution)/shard_map/pallas_call | solution.py:46
  61.2 0.7 collective-permute-done
  61.9 0.3 multiply_convert_fusion
  62.2 16.3 %all_to_all.10 = f16[4,96,1280]{2,1,0:T(8,128)(2,1)S(1)} all-to-all(f16[4,96,1280]{2,1,0:T(8,128)(2,1)S(1)} %bitcast.15), channel_id=1, replica_groups=mesh['zlo'=3,'y'=8,'x'=4,'zhi'=4,'core'=2] {'x'}, dimensions={0} | all-to-all | bytes 1966080 | tf_op jit(solution)/shard_map/all_to_all | solution.py:86
  78.4 0.0 copy-start.2
  78.4 0.1 convert_reduce_fusion
  78.6 24.5 %all_to_all.11 = f16[4,24,1280]{2,1,0:T(8,128)(2,1)S(1)} all-to-all(f16[4,24,1280]{2,1,0:T(8,128)(2,1)S(1)} %bitcast.17), channel_id=1, replica_groups=mesh['zlo'=3,'y'=8,'x'=4,'zhi'=4,'core'=2] {'zhi'}, dimensions={0} | all-to-all | bytes 491520 | tf_op jit(solution)/shard_map/all_to_all | solution.py:89
  103.1 0.0 copy-done.2
  103.2 0.7 multiply_add_fusion
  (2 shorter events, 0.1 us)
Async XLA Ops:
  40.7 2.1 %copy-start = (bf16[1280,1536]{1,0:T(8,128)(2,1)S(1)}, bf16[1280,1536]{1,0:T(8,128)(2,1)}, u32[]{:S(2)}) copy-start(bf16[1280,1536]{1,0:T(8,128)(2,1)} %ints_ref.3) | copy-start | bytes 11796484
  40.7 2.1 %copy-start.1 = (s32[20,24]{1,0:T(8,128)S(1)}, s32[20,24]{1,0:T(8,128)}, u32[]{:S(2)}) copy-start(s32[20,24]{1,0:T(8,128)} %tiles_ref.3) | copy-start | bytes 5764
  45.6 16.3 %collective-permute-start = (f32[384,1280]{1,0:T(8,128)S(1)}, f32[384,1280]{1,0:T(8,128)S(1)}, u32[]{:S(2)}, u32[]{:S(2)}) collective-permute-start(f32[384,1280]{1,0:T(8,128)S(1)} %shard_map.56), channel_id=1, source_target_pairs={{0,1},{1,0},{2,3},{3,2},{4,5},{5,4},{6,7},{7,6},{8,9},{9,8},{10,11... | collective-permute-start | bytes 5898248 | tf_op jit(solution)/shard_map/ppermute | solution.py:82
  78.4 24.7 %copy-start.2 = (f32[24,1280]{1,0:T(8,128)S(1)}, f32[24,1280]{1,0:T(8,128)}, u32[]{:S(2)}) copy-start(f32[24,1280]{1,0:T(8,128)} %param.9) | copy-start | bytes 368644

commit v2 on v1

v2 whole, which is shorter than its diff:
```python
import jax
import jax.numpy as jnp
from jax import lax
from jax.experimental import pallas as pl
from jax.experimental.pallas import tpu as pltpu
from jax.sharding import Mesh, PartitionSpec as P

AXES = ("zlo", "y", "x", "zhi", "core")
SIZES = (3, 8, 4, 4, 2)
ROW = ("zlo", "y")
COL = ("x", "zhi", "core")
TILE = 64
BLOCK = 256
PIECE = 128
VMEM_LIMIT = 24 * 2**20

AMP_SCALE = 2.0**13
X_SCALE = 2.0**6
Z_SCALE = 2.0**4


def dot(a, b):
    return lax.dot_general(a, b, (((1,), (1,)), ((), ())), preferred_element_type=jnp.float32)


def spread_flags(flags, width):
    count = flags.shape[1]
    tile_of = lax.shift_right_logical(
        lax.broadcasted_iota(jnp.int32, (count, width), 1), TILE.bit_length() - 1
    )
    spread = (tile_of == lax.broadcasted_iota(jnp.int32, (count, width), 0)).astype(jnp.bfloat16)
    return jnp.dot(flags.astype(jnp.bfloat16), spread, preferred_element_type=jnp.float32)


def masks_kernel(first_ref, amp_tiles_ref, int_tiles_ref, ints_ref, amp_mask_ref, masked_ref, spread_ref, flags_ref, sems):
    depth = amp_mask_ref.shape[1]
    pieces = [pl.ds(start, PIECE) for start in range(0, masked_ref.shape[0], PIECE)]
    flags_copy = pltpu.make_async_copy(int_tiles_ref, flags_ref, sems.at[len(pieces)])
    flags_copy.start()
    copies = [
        pltpu.make_async_copy(ints_ref.at[piece, :], masked_ref.at[piece, :], sems.at[at])
        for at, piece in enumerate(pieces)
    ]
    for copy in copies:
        copy.start()
    spread_ref[...] = spread_flags(amp_tiles_ref[...], depth) * AMP_SCALE
    parts = amp_mask_ref.shape[0]
    step = amp_tiles_ref.shape[0] // parts
    for part in range(parts):
        amp_mask_ref[part : part + 1, :] = spread_ref[pl.ds(part * step + first_ref[0], 1), :]
    flags_copy.wait()
    int_mask = spread_flags(flags_ref[...], depth).astype(jnp.bfloat16)
    for at, copy in enumerate(copies):
        copy.wait()
        for start in range(at * PIECE, (at + 1) * PIECE, TILE):
            rows = slice(start, start + TILE)
            tile = start // TILE
            masked_ref[rows, :] = masked_ref[rows, :] * int_mask[tile : tile + 1, :]


def masks(first, parts, amp_tiles, int_tiles, integrals):
    ab, depth = integrals.shape
    vmem, hbm = pl.BlockSpec(memory_space=pltpu.VMEM), pl.BlockSpec(memory_space=pltpu.HBM)
    return pl.pallas_call(
        masks_kernel,
        in_specs=[pl.BlockSpec(memory_space=pltpu.SMEM), vmem, hbm, hbm],
        out_specs=[vmem, vmem],
        out_shape=[
            jax.ShapeDtypeStruct((parts, depth), jnp.float32),
            jax.ShapeDtypeStruct((ab, depth), jnp.bfloat16),
        ],
        scratch_shapes=[
            pltpu.VMEM((amp_tiles.shape[0], depth), jnp.float32),
            pltpu.VMEM(int_tiles.shape, jnp.int32),
            pltpu.SemaphoreType.DMA((ab // PIECE + 1,)),
        ],
        compiler_params=pltpu.CompilerParams(vmem_limit_bytes=VMEM_LIMIT),
        cost_estimate=pl.CostEstimate(flops=ab * depth, bytes_accessed=4 * ab * depth, transcendentals=0),
    )(
        jnp.full((1,), first, jnp.int32),
        amp_tiles,
        pltpu.with_memory_space_constraint(int_tiles, pltpu.HBM),
        pltpu.with_memory_space_constraint(integrals, pltpu.HBM),
    )


def product_kernel(amps_ref, masked_ref, out_ref):
    for start in range(0, masked_ref.shape[0], BLOCK):
        block = slice(start, start + BLOCK)
        out_ref[:, block] = dot(amps_ref[...], masked_ref[block, :])


def product(amps, masked):
    rows, depth = amps.shape
    ab = masked.shape[0]
    vmem = pl.BlockSpec(memory_space=pltpu.VMEM)
    return pl.pallas_call(
        product_kernel,
        in_specs=[vmem, vmem],
        out_specs=vmem,
        out_shape=jax.ShapeDtypeStruct((rows, ab), jnp.float32),
        compiler_params=pltpu.CompilerParams(vmem_limit_bytes=VMEM_LIMIT),
        cost_estimate=pl.CostEstimate(
            flops=2 * rows * ab * depth, bytes_accessed=2 * (rows + ab) * depth + 4 * rows * ab, transcendentals=0
        ),
    )(amps, masked)


def sum_scatter(values, axis):
    sent = values.astype(jnp.float16)
    got = lax.all_to_all(sent, axis, 0, 0, tiled=True).astype(jnp.float32)
    return got.sum(0)


def on_device(amplitudes, amp_tiles, integrals, int_tiles, prior):
    f16, f32 = jnp.float16, jnp.float32
    local_rows, depth = amplitudes.shape
    ab = integrals.shape[0]
    own_rows = prior.shape[0]
    core, y = lax.axis_index("core"), lax.axis_index("y")
    n_x, n_zhi, n_core = lax.axis_size("x"), lax.axis_size("zhi"), lax.axis_size("core")

    zlo, n_zlo = lax.axis_index("zlo"), lax.axis_size("zlo")
    mask, masked = masks(y * local_rows // TILE, n_zlo, amp_tiles, int_tiles, integrals)
    held = [amplitudes]
    for hop in range(1, n_zlo):
        held.append(lax.ppermute(amplitudes, "zlo", [(i, (i + hop) % n_zlo) for i in range(n_zlo)]))
    near = []
    for source in range(n_zlo):
        block = held[0]
        for hop in range(1, n_zlo):
            block = jnp.where((zlo - hop) % n_zlo == source, held[hop], block)
        near.append(block)
    near = jnp.stack(near)
    near = (near.astype(f32) * mask[:, None, :]).astype(f16)
    amps = lax.all_gather(near, "y", axis=1, tiled=False)
    amps = amps.astype(jnp.bfloat16).reshape(n_x, n_zhi, n_core, own_rows, depth)
    amps = amps.transpose(2, 0, 1, 3, 4).reshape(n_core, n_x * n_zhi * own_rows, depth)

    other = product(lax.dynamic_index_in_dim(amps, 1 - core, 0, False), masked)
    crossing = lax.ppermute(other, "core", [(0, 1), (1, 0)])
    mine = product(lax.dynamic_index_in_dim(amps, core, 0, False), masked)
    total = (mine + crossing) * (X_SCALE / AMP_SCALE)
    total = sum_scatter(total.reshape(n_x, n_zhi * own_rows, ab), "x") * (Z_SCALE / X_SCALE)
    total = sum_scatter(total.reshape(n_zhi, own_rows, ab), "zhi")
    return prior + total * (1 / Z_SCALE)


def solution(mesh):
    parts = Mesh(mesh.devices.reshape(SIZES), AXES)
    in_specs = (P(ROW, COL), P(None, COL), P(ROW, COL), P(ROW, COL), P(COL, ROW))
    return jax.shard_map(
        on_device, mesh=parts, in_specs=in_specs, out_specs=P(COL, ROW), check_vma=False
    )
```

time: 106 us -> 102 us (0.962); the launches traced: 104 us -> 102 us
  blocking collectives: 79 us -> 70 us
  starting transfers between devices: 12.7 us -> 19.9 us
  waiting for transfers between devices: 0.7 us -> 3.39 us
  other arithmetic: 3.14 us -> 1.67 us
  local copies, waits for them, and re-layouts: 2.45 us -> 1.08 us
    all_gather x1 -> x0, blocking collectives: 10.8 us -> none  [on_device(): near = lax.all_gather(sent, 'zlo', axis=0, tiled=False)]
    ppermute x0 -> x2, starting transfers between devices: none -> 8.55 us  [on_device(): lax.ppermute(amplitudes, 'zlo', [(i, (i + hop) % n_zlo) for i in range(n_...]
    all_to_all x2, blocking collectives: 40.7 us -> 42.5 us  [sum_scatter(): got = lax.all_to_all(sent, axis, 0, 0, tiled=True).astype(jnp.float32)]
    ppermute x0 -> x2, waiting for transfers between devices: none -> 1.52 us  [on_device(): lax.ppermute(amplitudes, 'zlo', [(i, (i + hop) % n_zlo) for i in range(n_...]
    ppermute x1, starting transfers between devices: 12.7 us -> 11.4 us  [on_device(): crossing = lax.ppermute(other, 'core', [(0, 1), (1, 0)])]
    unnamed x6, local copies, waits for them, and re-layouts: 1.94 us -> 0.7 us
    ppermute x1, waiting for transfers between devices: 0.7 us -> 1.86 us  [on_device(): crossing = lax.ppermute(other, 'core', [(0, 1), (1, 0)])]
    pallas_call x2 -> x3, Pallas kernels: 5.71 us -> 5.65 us  [the longest x2 3.41 us: product(): pl.pallas_call(product_kernel, in_specs=[vmem, vmem], out_specs=vmem, out...]
  transfers between devices with their start and end apart: 1 -> 3, of which waited for: 1 -> 2; matrix products, arithmetic and copies ran while one was open for 0% -> 0% of each run, Pallas kernels for 3% -> 4%
where the time goes in v2:
time: 102 us
  blocking collectives  70 us (69%)
  starting transfers between devices  19.9 us (20%)
  Pallas kernels  5.65 us (6%)
  waiting for transfers between devices  3.39 us (3%)
  other arithmetic  1.67 us (2%)
  local copies, waits for them, and re-layouts  1.08 us (1%)
    all_to_all x2, blocking collectives, sum_scatter(): got = lax.all_to_all(sent, axis, 0, 0, tiled=True).astype(jnp.float32)  42.5 us
    all_gather x1, blocking collectives, on_device(): amps = lax.all_gather(near, 'y', axis=1, tiled=False)  27.5 us
    ppermute x1, starting transfers between devices, on_device(): crossing = lax.ppermute(other, 'core', [(0, 1), (1, 0)])  11.4 us
    ppermute x2, starting transfers between devices, on_device(): lax.ppermute(amplitudes, 'zlo', [(i, (i + hop) % n_zlo) for i in range(n_...  8.55 us
    pallas_call x2, Pallas kernels, product(): pl.pallas_call(product_kernel, in_specs=[vmem, vmem], out_specs=vmem, out...  3.41 us
    pallas_call x1, Pallas kernels, masks(): pl.pallas_call(masks_kernel, in_specs=[pl.BlockSpec(memory_space=pltpu.SM...  2.23 us
  transfers between devices with their start and end apart: 3, of which 2 were waited for; matrix products, arithmetic and copies ran while one was open for 0% of the time, Pallas kernels for 4%

profile of v2, /device:TPU:1, one launch (start us, length us, event | category | flops | bytes accessed | tf_op | source)
XLA Modules:
  0.0 101.9 jit_solution(18110819809271769049)
XLA Ops:
  0.0 6.6 %collective-permute-start = (bf16[32,1536]{1,0:T(8,128)(2,1)}, bf16[32,1536]{1,0:T(8,128)(2,1)S(1)}, u32[]{:S(2)}, u32[]{:S(2)}) collective-permute-start(bf16[32,1536]{1,0:T(8,128)(2,1)} %param.5), channel_id=1, source_target_pairs={{0,512},{256,0},{512,256},{1,513},{257,1},{513,257},{2,514},{258,2... | collective-permute-start | bytes 294920 | tf_op jit(solution)/shard_map/ppermute | solution.py:127
  6.6 1.9 %collective-permute-start.1 = (bf16[32,1536]{1,0:T(8,128)(2,1)}, bf16[32,1536]{1,0:T(8,128)(2,1)S(1)}, u32[]{:S(2)}, u32[]{:S(2)}) collective-permute-start(bf16[32,1536]{1,0:T(8,128)(2,1)} %param.5), channel_id=1, source_target_pairs={{0,256},{256,512},{512,0},{1,257},{257,513},{513,1},{2,258},{258,5... | collective-permute-start | bytes 294920 | tf_op jit(solution)/shard_map/ppermute | solution.py:127
  8.6 0.0 copy-start
  8.6 0.7 copy-done
  9.3 0.0 copy-start.2
  9.3 2.2 %shard_map.55 = (f32[3,1536]{1,0:T(4,128)S(1)}, bf16[1280,1536]{1,0:T(8,128)(2,1)S(1)}) custom-call(s32[1]{0:T(128)} %bitcast.3.first_ref, s32[12,24]{1,0:T(8,128)S(1)} %copy-done, s32[20,24]{1,0:T(8,128)} %int_tiles_ref.1, bf16[1280,1536]{1,0:T(8,128)(2,1)} %ints_ref.1), custom_call_target="tpu_custom_call" | custom-call | flops 1966080 | bytes 7864320 | tf_op jit(solution)/shard_map/pallas_call | solution.py:64
  11.6 0.0 collective-permute-done
  11.6 1.5 %collective-permute-done.1 = bf16[32,1536]{1,0:T(8,128)(2,1)S(1)} collective-permute-done((bf16[32,1536]{1,0:T(8,128)(2,1)}, bf16[32,1536]{1,0:T(8,128)(2,1)S(1)}, u32[]{:S(2)}, u32[]{:S(2)}) %collective-permute-start.1) | collective-permute-done | bytes 98336 | tf_op jit(solution)/shard_map/ppermute | solution.py:127
  13.1 0.0 copy-done.2
  13.1 0.1 multiply_convert_fusion.1
  13.2 27.5 %all-gather.1 = f16[3,8,32,1536]{3,2,1,0:T(8,128)(2,1)S(1)} all-gather(f16[3,1,32,1536]{3,2,1,0:T(8,128)(2,1)S(1)} %multiply_convert_fusion.1), channel_id=1, replica_groups=mesh['zlo'=3,'y'=8,'x'=4,'zhi'=4,'core'=2] {'y'}, dimensions={1}, use_global_device_ids=true | all-gather | bytes 2654208 | tf_op jit(solution)/shard_map/all_gather | solution.py:136
  40.7 0.4 convert_element_type.43
  41.2 0.2 copy.7
  41.4 0.2 dynamic-slice_bitcast_fusion
  41.6 1.7 %shard_map.57 = f32[384,1280]{1,0:T(8,128)S(1)} custom-call(bf16[384,1536]{1,0:T(8,128)(2,1)S(1)} %get-tuple-element.9.amps_ref, bf16[1280,1536]{1,0:T(8,128)(2,1)S(1)} %get-tuple-element.8.masked_ref), custom_call_target="tpu_custom_call" | custom-call | flops 1509949440 | bytes 7077888 | tf_op jit(solution)/shard_map/pallas_call | solution.py:97
  43.3 11.4 %collective-permute-start.2 = (f32[384,1280]{1,0:T(8,128)S(1)}, f32[384,1280]{1,0:T(8,128)S(1)}, u32[]{:S(2)}, u32[]{:S(2)}) collective-permute-start(f32[384,1280]{1,0:T(8,128)S(1)} %shard_map.57), channel_id=1, source_target_pairs={{0,1},{1,0},{2,3},{3,2},{4,5},{5,4},{6,7},{7,6},{8,9},{9,8},{10,11... | collective-permute-start | bytes 5898248 | tf_op jit(solution)/shard_map/ppermute | solution.py:141
  54.7 1.7 %shard_map.56 = f32[384,1280]{1,0:T(8,128)S(1)} custom-call(bf16[384,1536]{1,0:T(8,128)(2,1)S(1)} %get-tuple-element.10.amps_ref, bf16[1280,1536]{1,0:T(8,128)(2,1)S(1)} %get-tuple-element.8.masked_ref), custom_call_target="tpu_custom_call" | custom-call | flops 1509949440 | bytes 7077888 | tf_op jit(solution)/shard_map/pallas_call | solution.py:97
  56.4 1.9 %collective-permute-done.2 = f32[384,1280]{1,0:T(8,128)S(1)} collective-permute-done((f32[384,1280]{1,0:T(8,128)S(1)}, f32[384,1280]{1,0:T(8,128)S(1)}, u32[]{:S(2)}, u32[]{:S(2)}) %collective-permute-start.2) | collective-permute-done | bytes 1966112 | tf_op jit(solution)/shard_map/ppermute | solution.py:141
  58.3 0.3 multiply_convert_fusion
  58.5 16.3 %all_to_all.10 = f16[4,96,1280]{2,1,0:T(8,128)(2,1)S(1)} all-to-all(f16[4,96,1280]{2,1,0:T(8,128)(2,1)S(1)} %bitcast.19), channel_id=1, replica_groups=mesh['zlo'=3,'y'=8,'x'=4,'zhi'=4,'core'=2] {'x'}, dimensions={0} | all-to-all | bytes 1966080 | tf_op jit(solution)/shard_map/all_to_all | solution.py:111
  74.8 0.0 copy-start.1
  74.8 0.1 convert_reduce_fusion
  75.0 26.2 %all_to_all.11 = f16[4,24,1280]{2,1,0:T(8,128)(2,1)S(1)} all-to-all(f16[4,24,1280]{2,1,0:T(8,128)(2,1)S(1)} %bitcast.20), channel_id=1, replica_groups=mesh['zlo'=3,'y'=8,'x'=4,'zhi'=4,'core'=2] {'zhi'}, dimensions={0} | all-to-all | bytes 491520 | tf_op jit(solution)/shard_map/all_to_all | solution.py:111
  101.3 0.0 copy-done.1
  101.3 0.7 multiply_add_fusion
  (3 shorter events, 0.1 us)
Async XLA Ops:
  0.0 11.6 %collective-permute-start = (bf16[32,1536]{1,0:T(8,128)(2,1)}, bf16[32,1536]{1,0:T(8,128)(2,1)S(1)}, u32[]{:S(2)}, u32[]{:S(2)}) collective-permute-start(bf16[32,1536]{1,0:T(8,128)(2,1)} %param.5), channel_id=1, source_target_pairs={{0,512},{256,0},{512,256},{1,513},{257,1},{513,257},{2,514},{258,2... | collective-permute-start | bytes 294920 | tf_op jit(solution)/shard_map/ppermute | solution.py:127
  6.6 6.5 %collective-permute-start.1 = (bf16[32,1536]{1,0:T(8,128)(2,1)}, bf16[32,1536]{1,0:T(8,128)(2,1)S(1)}, u32[]{:S(2)}, u32[]{:S(2)}) collective-permute-start(bf16[32,1536]{1,0:T(8,128)(2,1)} %param.5), channel_id=1, source_target_pairs={{0,256},{256,512},{512,0},{1,257},{257,513},{513,1},{2,258},{258,5... | collective-permute-start | bytes 294920 | tf_op jit(solution)/shard_map/ppermute | solution.py:127
  8.6 0.7 copy-start
  9.3 3.8 %copy-start.2 = (bf16[32,1536]{1,0:T(8,128)(2,1)S(1)}, bf16[32,1536]{1,0:T(8,128)(2,1)}, u32[]{:S(2)}) copy-start(bf16[32,1536]{1,0:T(8,128)(2,1)} %param.5) | copy-start | bytes 294916
  43.3 15.0 %collective-permute-start.2 = (f32[384,1280]{1,0:T(8,128)S(1)}, f32[384,1280]{1,0:T(8,128)S(1)}, u32[]{:S(2)}, u32[]{:S(2)}) collective-permute-start(f32[384,1280]{1,0:T(8,128)S(1)} %shard_map.57), channel_id=1, source_target_pairs={{0,1},{1,0},{2,3},{3,2},{4,5},{5,4},{6,7},{7,6},{8,9},{9,8},{10,11... | collective-permute-start | bytes 5898248 | tf_op jit(solution)/shard_map/ppermute | solution.py:141
  74.8 26.5 %copy-start.1 = (f32[24,1280]{1,0:T(8,128)S(1)}, f32[24,1280]{1,0:T(8,128)}, u32[]{:S(2)}) copy-start(f32[24,1280]{1,0:T(8,128)} %param.9) | copy-start | bytes 368644

commit v3 on v2

--- a/solution.py
+++ b/solution.py
@@ -134,12 +134,14 @@
     near = jnp.stack(near)
     near = (near.astype(f32) * mask[:, None, :]).astype(f16)
     amps = lax.all_gather(near, "y", axis=1, tiled=False)
-    amps = amps.astype(jnp.bfloat16).reshape(n_x, n_zhi, n_core, own_rows, depth)
-    amps = amps.transpose(2, 0, 1, 3, 4).reshape(n_core, n_x * n_zhi * own_rows, depth)
+    amps = amps.reshape(n_x, n_zhi, n_core, own_rows, depth)
 
-    other = product(lax.dynamic_index_in_dim(amps, 1 - core, 0, False), masked)
-    crossing = lax.ppermute(other, "core", [(0, 1), (1, 0)])
-    mine = product(lax.dynamic_index_in_dim(amps, core, 0, False), masked)
+    def product_of(c):
+        rows = lax.dynamic_index_in_dim(amps, c, 2, False).astype(jnp.bfloat16)
+        return product(rows.reshape(n_x * n_zhi * own_rows, depth), masked)
+
+    crossing = lax.ppermute(product_of(1 - core), "core", [(0, 1), (1, 0)])
+    mine = product_of(core)
     total = (mine + crossing) * (X_SCALE / AMP_SCALE)
     total = sum_scatter(total.reshape(n_x, n_zhi * own_rows, ab), "x") * (Z_SCALE / X_SCALE)
     total = sum_scatter(total.reshape(n_zhi, own_rows, ab), "zhi")

time: 102 us -> 102 us (level)
  no operation moved by 1% of the time
where the time goes in v3:
time: 102 us
  blocking collectives  70 us (69%)
  starting transfers between devices  19.9 us (20%)
  Pallas kernels  5.65 us (6%)
  waiting for transfers between devices  3.39 us (3%)
  other arithmetic  1.72 us (2%)
    all_to_all x2, blocking collectives, sum_scatter(): got = lax.all_to_all(sent, axis, 0, 0, tiled=True).astype(jnp.float32)  42.5 us
    all_gather x1, blocking collectives, on_device(): amps = lax.all_gather(near, 'y', axis=1, tiled=False)  27.5 us
    ppermute x1, starting transfers between devices, on_device(): crossing = lax.ppermute(product_of(1 - core), 'core', [(0, 1), (1, 0)])  11.4 us
    ppermute x2, starting transfers between devices, on_device(): lax.ppermute(amplitudes, 'zlo', [(i, (i + hop) % n_zlo) for i in range(n_...  8.55 us
    pallas_call x2, Pallas kernels, product(): pl.pallas_call(product_kernel, in_specs=[vmem, vmem], out_specs=vmem, out...  3.42 us
    pallas_call x1, Pallas kernels, masks(): pl.pallas_call(masks_kernel, in_specs=[pl.BlockSpec(memory_space=pltpu.SM...  2.23 us
  transfers between devices with their start and end apart: 3, of which 2 were waited for; matrix products, arithmetic and copies ran while one was open for 0% of the time, Pallas kernels for 4%

profile of v3, /device:TPU:1, one launch (start us, length us, event | category | flops | bytes accessed | tf_op | source)
XLA Modules:
  0.0 101.6 jit_solution(13839129741224350507)
XLA Ops:
  0.0 6.6 %collective-permute-start = (bf16[32,1536]{1,0:T(8,128)(2,1)}, bf16[32,1536]{1,0:T(8,128)(2,1)S(1)}, u32[]{:S(2)}, u32[]{:S(2)}) collective-permute-start(bf16[32,1536]{1,0:T(8,128)(2,1)} %param.5), channel_id=1, source_target_pairs={{0,512},{256,0},{512,256},{1,513},{257,1},{513,257},{2,514},{258,2... | collective-permute-start | bytes 294920 | tf_op jit(solution)/shard_map/ppermute | solution.py:127
  6.6 1.9 %collective-permute-start.1 = (bf16[32,1536]{1,0:T(8,128)(2,1)}, bf16[32,1536]{1,0:T(8,128)(2,1)S(1)}, u32[]{:S(2)}, u32[]{:S(2)}) collective-permute-start(bf16[32,1536]{1,0:T(8,128)(2,1)} %param.5), channel_id=1, source_target_pairs={{0,256},{256,512},{512,0},{1,257},{257,513},{513,1},{2,258},{258,5... | collective-permute-start | bytes 294920 | tf_op jit(solution)/shard_map/ppermute | solution.py:127
  8.6 0.0 copy-start
  8.6 0.7 copy-done
  9.3 0.0 copy-start.2
  9.3 2.2 %shard_map.55 = (f32[3,1536]{1,0:T(4,128)S(1)}, bf16[1280,1536]{1,0:T(8,128)(2,1)S(1)}) custom-call(s32[1]{0:T(128)} %bitcast.3.first_ref, s32[12,24]{1,0:T(8,128)S(1)} %copy-done, s32[20,24]{1,0:T(8,128)} %int_tiles_ref.1, bf16[1280,1536]{1,0:T(8,128)(2,1)} %ints_ref.1), custom_call_target="tpu_custom_call" | custom-call | flops 1966080 | bytes 7864320 | tf_op jit(solution)/shard_map/pallas_call | solution.py:64
  11.6 0.0 collective-permute-done
  11.6 1.5 %collective-permute-done.1 = bf16[32,1536]{1,0:T(8,128)(2,1)S(1)} collective-permute-done((bf16[32,1536]{1,0:T(8,128)(2,1)}, bf16[32,1536]{1,0:T(8,128)(2,1)S(1)}, u32[]{:S(2)}, u32[]{:S(2)}) %collective-permute-start.1) | collective-permute-done | bytes 98336 | tf_op jit(solution)/shard_map/ppermute | solution.py:127
  13.1 0.0 copy-done.2
  13.1 0.1 multiply_convert_fusion.1
  13.2 27.5 %all-gather.1 = f16[3,8,32,1536]{3,2,1,0:T(8,128)(2,1)S(1)} all-gather(f16[3,1,32,1536]{3,2,1,0:T(8,128)(2,1)S(1)} %multiply_convert_fusion.1), channel_id=1, replica_groups=mesh['zlo'=3,'y'=8,'x'=4,'zhi'=4,'core'=2] {'y'}, dimensions={1}, use_global_device_ids=true | all-gather | bytes 2654208 | tf_op jit(solution)/shard_map/all_gather | solution.py:136
  40.7 0.5 bitcast_convert_fusion
  41.2 1.7 %shard_map.57 = f32[384,1280]{1,0:T(8,128)S(1)} custom-call(bf16[384,1536]{1,0:T(8,128)(2,1)S(1)} %bitcast.17, bf16[1280,1536]{1,0:T(8,128)(2,1)S(1)} %get-tuple-element.8.masked_ref), custom_call_target="tpu_custom_call" | custom-call | flops 1509949440 | bytes 7077888 | tf_op jit(solution)/shard_map/pallas_call | solution.py:97
  43.0 11.4 %collective-permute-start.2 = (f32[384,1280]{1,0:T(8,128)S(1)}, f32[384,1280]{1,0:T(8,128)S(1)}, u32[]{:S(2)}, u32[]{:S(2)}) collective-permute-start(f32[384,1280]{1,0:T(8,128)S(1)} %shard_map.57), channel_id=1, source_target_pairs={{0,1},{1,0},{2,3},{3,2},{4,5},{5,4},{6,7},{7,6},{8,9},{9,8},{10,11... | collective-permute-start | bytes 5898248 | tf_op jit(solution)/shard_map/ppermute | solution.py:143
  54.4 1.7 %shard_map.56 = f32[384,1280]{1,0:T(8,128)S(1)} custom-call(bf16[384,1536]{1,0:T(8,128)(2,1)S(1)} %bitcast.16, bf16[1280,1536]{1,0:T(8,128)(2,1)S(1)} %get-tuple-element.8.masked_ref), custom_call_target="tpu_custom_call" | custom-call | flops 1509949440 | bytes 7077888 | tf_op jit(solution)/shard_map/pallas_call | solution.py:97
  56.1 1.9 %collective-permute-done.2 = f32[384,1280]{1,0:T(8,128)S(1)} collective-permute-done((f32[384,1280]{1,0:T(8,128)S(1)}, f32[384,1280]{1,0:T(8,128)S(1)}, u32[]{:S(2)}, u32[]{:S(2)}) %collective-permute-start.2) | collective-permute-done | bytes 1966112 | tf_op jit(solution)/shard_map/ppermute | solution.py:143
  57.9 0.3 multiply_convert_fusion
  58.2 16.3 %all_to_all.10 = f16[4,96,1280]{2,1,0:T(8,128)(2,1)S(1)} all-to-all(f16[4,96,1280]{2,1,0:T(8,128)(2,1)S(1)} %bitcast.19), channel_id=1, replica_groups=mesh['zlo'=3,'y'=8,'x'=4,'zhi'=4,'core'=2] {'x'}, dimensions={0} | all-to-all | bytes 1966080 | tf_op jit(solution)/shard_map/all_to_all | solution.py:111
  74.4 0.0 copy-start.1
  74.5 0.1 convert_reduce_fusion
  74.6 26.2 %all_to_all.11 = f16[4,24,1280]{2,1,0:T(8,128)(2,1)S(1)} all-to-all(f16[4,24,1280]{2,1,0:T(8,128)(2,1)S(1)} %bitcast.20), channel_id=1, replica_groups=mesh['zlo'=3,'y'=8,'x'=4,'zhi'=4,'core'=2] {'zhi'}, dimensions={0} | all-to-all | bytes 491520 | tf_op jit(solution)/shard_map/all_to_all | solution.py:111
  100.9 0.0 copy-done.1
  100.9 0.7 multiply_add_fusion
  (3 shorter events, 0.1 us)
Async XLA Ops:
  0.0 11.6 %collective-permute-start = (bf16[32,1536]{1,0:T(8,128)(2,1)}, bf16[32,1536]{1,0:T(8,128)(2,1)S(1)}, u32[]{:S(2)}, u32[]{:S(2)}) collective-permute-start(bf16[32,1536]{1,0:T(8,128)(2,1)} %param.5), channel_id=1, source_target_pairs={{0,512},{256,0},{512,256},{1,513},{257,1},{513,257},{2,514},{258,2... | collective-permute-start | bytes 294920 | tf_op jit(solution)/shard_map/ppermute | solution.py:127
  6.6 6.5 %collective-permute-start.1 = (bf16[32,1536]{1,0:T(8,128)(2,1)}, bf16[32,1536]{1,0:T(8,128)(2,1)S(1)}, u32[]{:S(2)}, u32[]{:S(2)}) collective-permute-start(bf16[32,1536]{1,0:T(8,128)(2,1)} %param.5), channel_id=1, source_target_pairs={{0,256},{256,512},{512,0},{1,257},{257,513},{513,1},{2,258},{258,5... | collective-permute-start | bytes 294920 | tf_op jit(solution)/shard_map/ppermute | solution.py:127
  8.6 0.7 copy-start
  9.3 3.8 %copy-start.2 = (bf16[32,1536]{1,0:T(8,128)(2,1)S(1)}, bf16[32,1536]{1,0:T(8,128)(2,1)}, u32[]{:S(2)}) copy-start(bf16[32,1536]{1,0:T(8,128)(2,1)} %param.5) | copy-start | bytes 294916
  43.0 15.0 %collective-permute-start.2 = (f32[384,1280]{1,0:T(8,128)S(1)}, f32[384,1280]{1,0:T(8,128)S(1)}, u32[]{:S(2)}, u32[]{:S(2)}) collective-permute-start(f32[384,1280]{1,0:T(8,128)S(1)} %shard_map.57), channel_id=1, source_target_pairs={{0,1},{1,0},{2,3},{3,2},{4,5},{5,4},{6,7},{7,6},{8,9},{9,8},{10,11... | collective-permute-start | bytes 5898248 | tf_op jit(solution)/shard_map/ppermute | solution.py:143
  74.4 26.5 %copy-start.1 = (f32[24,1280]{1,0:T(8,128)S(1)}, f32[24,1280]{1,0:T(8,128)}, u32[]{:S(2)}) copy-start(f32[24,1280]{1,0:T(8,128)} %param.9) | copy-start | bytes 368644

commit v4 on v3

--- a/solution.py
+++ b/solution.py
@@ -122,9 +122,12 @@
 
     zlo, n_zlo = lax.axis_index("zlo"), lax.axis_size("zlo")
     mask, masked = masks(y * local_rows // TILE, n_zlo, amp_tiles, int_tiles, integrals)
-    held = [amplitudes]
-    for hop in range(1, n_zlo):
-        held.append(lax.ppermute(amplitudes, "zlo", [(i, (i + hop) % n_zlo) for i in range(n_zlo)]))
+    def send(turn):
+        pairs = [(2 * i + c, (i + (turn if c == 0 else n_zlo - turn)) % n_zlo * 2 + c) for i in range(n_zlo) for c in range(2)]
+        return lax.ppermute(amplitudes, ("zlo", "core"), pairs)
+
+    sent = [send(turn) for turn in range(1, n_zlo)]
+    held = [amplitudes] + [jnp.where(core == 0, a, b) for a, b in zip(sent, sent[::-1])]
     near = []
     for source in range(n_zlo):
         block = held[0]

time: 102 us -> 101 us (level)
  the two profiles are of different devices: /device:TPU:1 before, /device:TPU:8 now
where the time goes in v4:
time: 101 us
  blocking collectives  79.4 us (79%)
  starting transfers between devices  9.92 us (10%)
  Pallas kernels  5.66 us (6%)
  waiting for transfers between devices  3.1 us (3%)
  other arithmetic  1.74 us (2%)
    all_to_all x2, blocking collectives, sum_scatter(): got = lax.all_to_all(sent, axis, 0, 0, tiled=True).astype(jnp.float32)  43.4 us
    all_gather x1, blocking collectives, on_device(): amps = lax.all_gather(near, 'y', axis=1, tiled=False)  35.9 us
    ppermute x2, starting transfers between devices, send(): return lax.ppermute(amplitudes, ('zlo', 'core'), pairs)  8 us
    pallas_call x2, Pallas kernels, product(): pl.pallas_call(product_kernel, in_specs=[vmem, vmem], out_specs=vmem, out...  3.43 us
    pallas_call x1, Pallas kernels, masks(): pl.pallas_call(masks_kernel, in_specs=[pl.BlockSpec(memory_space=pltpu.SM...  2.23 us
    ppermute x1, waiting for transfers between devices, on_device(): crossing = lax.ppermute(product_of(1 - core), 'core', [(0, 1), (1, 0)])  2.22 us
  transfers between devices with their start and end apart: 3, of which 2 were waited for; matrix products, arithmetic and copies ran while one was open for 0% of the time, Pallas kernels for 4%

profile of v4, /device:TPU:8, one launch (start us, length us, event | category | flops | bytes accessed | tf_op | source)
XLA Modules:
  0.0 100.7 jit_solution(13182712720761544151)
XLA Ops:
  0.0 4.3 %collective-permute-start.1 = (bf16[32,1536]{1,0:T(8,128)(2,1)}, bf16[32,1536]{1,0:T(8,128)(2,1)S(1)}, u32[]{:S(2)}, u32[]{:S(2)}) collective-permute-start(bf16[32,1536]{1,0:T(8,128)(2,1)} %param.5), channel_id=1, source_target_pairs={{0,256},{1,513},{256,512},{257,1},{512,0},{513,257},{2,258},{3,515... | collective-permute-start | bytes 294920 | tf_op jit(solution)/shard_map/ppermute | solution.py:127
  4.3 3.7 %collective-permute-start = (bf16[32,1536]{1,0:T(8,128)(2,1)}, bf16[32,1536]{1,0:T(8,128)(2,1)S(1)}, u32[]{:S(2)}, u32[]{:S(2)}) collective-permute-start(bf16[32,1536]{1,0:T(8,128)(2,1)} %param.5), channel_id=1, source_target_pairs={{0,512},{1,257},{256,0},{257,513},{512,256},{513,1},{2,514},{3,259... | collective-permute-start | bytes 294920 | tf_op jit(solution)/shard_map/ppermute | solution.py:127
  8.1 0.0 copy-start
  8.1 0.7 copy-done
  8.8 0.0 copy-start.1
  8.8 2.2 %shard_map.55 = (f32[3,1536]{1,0:T(4,128)S(1)}, bf16[1280,1536]{1,0:T(8,128)(2,1)S(1)}) custom-call(s32[1]{0:T(128)} %bitcast.3.first_ref, s32[12,24]{1,0:T(8,128)S(1)} %copy-done, s32[20,24]{1,0:T(8,128)} %int_tiles_ref.1, bf16[1280,1536]{1,0:T(8,128)(2,1)} %ints_ref.1), custom_call_target="tpu_custom_call" | custom-call | flops 1966080 | bytes 7864320 | tf_op jit(solution)/shard_map/pallas_call | solution.py:64
  11.0 0.0 collective-permute-done.1
  11.0 0.9 collective-permute-done
  11.9 0.0 copy-done.1
  12.0 0.1 multiply_convert_fusion.1
  12.1 35.9 %all-gather.1 = f16[3,8,32,1536]{3,2,1,0:T(8,128)(2,1)S(1)} all-gather(f16[3,1,32,1536]{3,2,1,0:T(8,128)(2,1)S(1)} %multiply_convert_fusion.1), channel_id=1, replica_groups=mesh['zlo'=3,'y'=8,'x'=4,'zhi'=4,'core'=2] {'y'}, dimensions={1}, use_global_device_ids=true | all-gather | bytes 2654208 | tf_op jit(solution)/shard_map/all_gather | solution.py:139
  48.0 0.5 bitcast_convert_fusion
  48.5 1.7 %shard_map.57 = f32[384,1280]{1,0:T(8,128)S(1)} custom-call(bf16[384,1536]{1,0:T(8,128)(2,1)S(1)} %bitcast.17, bf16[1280,1536]{1,0:T(8,128)(2,1)S(1)} %get-tuple-element.8.masked_ref), custom_call_target="tpu_custom_call" | custom-call | flops 1509949440 | bytes 7077888 | tf_op jit(solution)/shard_map/pallas_call | solution.py:97
  50.2 1.9 %collective-permute-start.2 = (f32[384,1280]{1,0:T(8,128)S(1)}, f32[384,1280]{1,0:T(8,128)S(1)}, u32[]{:S(2)}, u32[]{:S(2)}) collective-permute-start(f32[384,1280]{1,0:T(8,128)S(1)} %shard_map.57), channel_id=1, source_target_pairs={{0,1},{1,0},{2,3},{3,2},{4,5},{5,4},{6,7},{7,6},{8,9},{9,8},{10,11... | collective-permute-start | bytes 5898248 | tf_op jit(solution)/shard_map/ppermute | solution.py:146
  52.1 1.7 %shard_map.56 = f32[384,1280]{1,0:T(8,128)S(1)} custom-call(bf16[384,1536]{1,0:T(8,128)(2,1)S(1)} %bitcast.16, bf16[1280,1536]{1,0:T(8,128)(2,1)S(1)} %get-tuple-element.8.masked_ref), custom_call_target="tpu_custom_call" | custom-call | flops 1509949440 | bytes 7077888 | tf_op jit(solution)/shard_map/pallas_call | solution.py:97
  53.9 2.2 %collective-permute-done.2 = f32[384,1280]{1,0:T(8,128)S(1)} collective-permute-done((f32[384,1280]{1,0:T(8,128)S(1)}, f32[384,1280]{1,0:T(8,128)S(1)}, u32[]{:S(2)}, u32[]{:S(2)}) %collective-permute-start.2) | collective-permute-done | bytes 1966112 | tf_op jit(solution)/shard_map/ppermute | solution.py:146
  56.1 0.3 multiply_convert_fusion
  56.3 17.4 %all_to_all.10 = f16[4,96,1280]{2,1,0:T(8,128)(2,1)S(1)} all-to-all(f16[4,96,1280]{2,1,0:T(8,128)(2,1)S(1)} %bitcast.19), channel_id=1, replica_groups=mesh['zlo'=3,'y'=8,'x'=4,'zhi'=4,'core'=2] {'x'}, dimensions={0} | all-to-all | bytes 1966080 | tf_op jit(solution)/shard_map/all_to_all | solution.py:111
  73.7 0.0 copy-start.2
  73.7 0.1 convert_reduce_fusion
  73.9 26.1 %all_to_all.11 = f16[4,24,1280]{2,1,0:T(8,128)(2,1)S(1)} all-to-all(f16[4,24,1280]{2,1,0:T(8,128)(2,1)S(1)} %bitcast.20), channel_id=1, replica_groups=mesh['zlo'=3,'y'=8,'x'=4,'zhi'=4,'core'=2] {'zhi'}, dimensions={0} | all-to-all | bytes 491520 | tf_op jit(solution)/shard_map/all_to_all | solution.py:111
  100.0 0.0 copy-done.2
  100.0 0.7 multiply_add_fusion
  (4 shorter events, 0.1 us)
Async XLA Ops:
  0.0 11.0 %collective-permute-start.1 = (bf16[32,1536]{1,0:T(8,128)(2,1)}, bf16[32,1536]{1,0:T(8,128)(2,1)S(1)}, u32[]{:S(2)}, u32[]{:S(2)}) collective-permute-start(bf16[32,1536]{1,0:T(8,128)(2,1)} %param.5), channel_id=1, source_target_pairs={{0,256},{1,513},{256,512},{257,1},{512,0},{513,257},{2,258},{3,515... | collective-permute-start | bytes 294920 | tf_op jit(solution)/shard_map/ppermute | solution.py:127
  4.3 7.6 %collective-permute-start = (bf16[32,1536]{1,0:T(8,128)(2,1)}, bf16[32,1536]{1,0:T(8,128)(2,1)S(1)}, u32[]{:S(2)}, u32[]{:S(2)}) collective-permute-start(bf16[32,1536]{1,0:T(8,128)(2,1)} %param.5), channel_id=1, source_target_pairs={{0,512},{1,257},{256,0},{257,513},{512,256},{513,1},{2,514},{3,259... | collective-permute-start | bytes 294920 | tf_op jit(solution)/shard_map/ppermute | solution.py:127
  8.1 0.7 copy-start
  8.8 3.1 %copy-start.1 = (bf16[32,1536]{1,0:T(8,128)(2,1)S(1)}, bf16[32,1536]{1,0:T(8,128)(2,1)}, u32[]{:S(2)}) copy-start(bf16[32,1536]{1,0:T(8,128)(2,1)} %param.5) | copy-start | bytes 294916
  50.2 5.9 %collective-permute-start.2 = (f32[384,1280]{1,0:T(8,128)S(1)}, f32[384,1280]{1,0:T(8,128)S(1)}, u32[]{:S(2)}, u32[]{:S(2)}) collective-permute-start(f32[384,1280]{1,0:T(8,128)S(1)} %shard_map.57), channel_id=1, source_target_pairs={{0,1},{1,0},{2,3},{3,2},{4,5},{5,4},{6,7},{7,6},{8,9},{9,8},{10,11... | collective-permute-start | bytes 5898248 | tf_op jit(solution)/shard_map/ppermute | solution.py:146
  73.7 26.3 %copy-start.2 = (f32[24,1280]{1,0:T(8,128)S(1)}, f32[24,1280]{1,0:T(8,128)}, u32[]{:S(2)}) copy-start(f32[24,1280]{1,0:T(8,128)} %param.9) | copy-start | bytes 368644
